TPU v7x, 1024 devices: a whole 4x8x16 slice. The times are simulated.
1024 devices in a mesh: dp: 256 (over y, z, core), tp: 4 (over x).
Axes of the slice: x: 4, y: 8, z: 16, core: 2. Of those that a mesh axis runs over, the one named last changes fastest.
Arguments:
- hidden: bfloat16 [256, 128, 7168], P('dp', None, 'tp'), may hold values from -6 to 6
- routes: int32 [256, 1], P('dp'), may hold values from 0 to 2, as said below
- counts: int32 [256, 1], P('dp'), may hold values from 64 to 128
- gain_in: float32 [7168], P('tp'), may hold values from 0.1 to 1.9
- kv_down: bfloat16 [7168, 256], P('tp'), may hold values from -0.0625 to 0.0625
- gain_latent: float32 [256], replicated, may hold values from 0.1 to 1.9
- cotangent: bfloat16 [256, 3, 1, 128, 256], P('dp'), may hold values from -0.25 to 0.25
Outputs:
- latent: bfloat16 [256, 3, 1, 128, 256], P('dp')
- gradient: float32 [256, 7168], P('dp', 'tp')
Inputs may be any that keep to these rules, and one draw needn't show every extreme that they name: `routes`: every offset sends a panel's trainer to a server at most 2 places further along dp, wrapping around; loads over trainers are uneven.
All inputs are finite; a program needn't handle non-finite values.
Results may differ from a plain program's by a relative error of at most 0.005.
Values may be sent and summed in bfloat16 or wider, within the bound.
No kernel may reach another device: no remote copies, remote signals or barrier semaphores. Data moves between devices by JAX's collectives and lax.ppermute only.
A program may use at most 32 MiB of HBM per device.

v0:
```python
import jax
import jax.numpy as jnp
from jax import lax
from jax.sharding import PartitionSpec as P

REACH = 3


epsilon = 1e-06


def from_behind(shard, axis, by):
    devices = lax.axis_size(axis)
    return lax.ppermute(shard, axis, [(i, (i + by) % devices) for i in range(devices)])


def finish(raw, gain_latent, cotangent_rows, valid_mask):
    rms_lat = jnp.sqrt(jnp.mean(raw * raw, axis=-1) + epsilon)
    unit_rows = raw / rms_lat[:, None]
    normed = (unit_rows * gain_latent * valid_mask[:, None]).astype(jnp.bfloat16)
    weighted = gain_latent * (cotangent_rows.astype(jnp.float32) * valid_mask[:, None])
    latent_grad = (
        weighted - unit_rows * jnp.mean(unit_rows * weighted, axis=-1, keepdims=True)
    ) / rms_lat[:, None]
    backward = latent_grad.astype(jnp.bfloat16)
    return (normed, backward)


def panel_work(blocks, limits, gain_in, kv_down, gain_latent, cotangents):
    panel_count = blocks.shape[0]
    panel_len = blocks.shape[1]
    total_rows = panel_count * panel_len
    latent_width = kv_down.shape[1]
    widened = blocks.reshape(total_rows, blocks.shape[2]).astype(jnp.float32)
    scaled = (widened * gain_in).astype(jnp.bfloat16)
    partial_value = jnp.dot(scaled, kv_down, preferred_element_type=jnp.float32)
    position = lax.broadcasted_iota(jnp.int32, (panel_count, panel_len), 1).astype(jnp.float32)
    valid_mask = (position < limits[:, None]).astype(jnp.float32).reshape(total_rows)
    cotangent_rows = cotangents.reshape(total_rows, latent_width)
    summed = lax.psum(partial_value, "tp")
    normed, backward = finish(summed, gain_latent, cotangent_rows, valid_mask)
    return (normed.reshape(panel_count, panel_len, latent_width), backward, scaled)


def body(hidden, routes, counts, gain_in, kv_down, gain_latent, cotangent):
    own_routes = routes[0]
    own_counts = counts[0]
    slot_count = hidden.shape[0]
    panel_len = hidden.shape[1]
    latent_width = kv_down.shape[1]
    arrived_blocks = []
    arrived_limits = []
    for offset in range(REACH):
        sent_counts = jnp.where(own_routes == offset, own_counts, 0).astype(jnp.bfloat16)
        if offset == 0:
            arrived_panels, arrived_counts = (hidden, sent_counts)
        else:
            arrived_panels, arrived_counts = from_behind((hidden, sent_counts), "dp", offset)
        arrived_blocks.append(arrived_panels)
        arrived_limits.append(arrived_counts.astype(jnp.float32))
    blocks = jnp.concatenate(arrived_blocks, axis=0)
    limits = jnp.concatenate(arrived_limits, axis=0)
    cotangents = cotangent[0].reshape(REACH * slot_count, panel_len, latent_width)
    normed, backward, scaled = panel_work(blocks, limits, gain_in, kv_down, gain_latent, cotangents)
    latent = normed.reshape(1, REACH, slot_count, panel_len, latent_width)
    gradient = lax.psum_scatter(
        lax.dot_general(
            backward, scaled, (((0,), (0,)), ((), ())), preferred_element_type=jnp.float32
        ),
        "dp",
        scatter_dimension=0,
        tiled=True,
    )
    return (latent, gradient)


def solution(mesh):
    in_specs = (
        P("dp", None, "tp"),
        P("dp", None),
        P("dp", None),
        P("tp"),
        P("tp", None),
        P(),
        P("dp", None, None, None, None),
    )
    out_specs = (P("dp", None, None, None, None), P("dp", "tp"))
    return jax.shard_map(body, mesh=mesh, in_specs=in_specs, out_specs=out_specs, check_vma=False)
```

profile of v0, /device:TPU:30, one launch (start us, length us, event | category | flops | bytes accessed | tf_op | source)
XLA Modules:
  0.0 477.1 jit_solution(17787616040476870219)
XLA Ops:
  7.2 0.0 copy-start
  7.2 0.0 all-reduce.4.cloned.1.call-start
  7.2 4.4 collective-permute-start.1
  11.6 1.9 collective-permute-start
  14.9 8.0 %collective-permute-start.3 = (bf16[1]{0:T(256)(128)(2,1)}, bf16[1]{0:T(256)(128)(2,1)}, u32[]{:S(2)}, u32[]{:S(2)}) collective-permute-start(bf16[1]{0:T(256)(128)(2,1)} %bitcast.3), channel_id=1, source_target_pairs={{0,8},{4,12},{8,16},{12,20},{16,24},{20,28},{24,32},{28,36},{32,40... | collective-permute-start | bytes 14 | tf_op jit(solution)/shard_map/ppermute | solution.py:14
  22.9 6.6 %collective-permute-start.2 = (bf16[1]{0:T(256)(128)(2,1)}, bf16[1]{0:T(256)(128)(2,1)}, u32[]{:S(2)}, u32[]{:S(2)}) collective-permute-start(bf16[1]{0:T(256)(128)(2,1)} %bitcast.2), channel_id=1, source_target_pairs={{0,4},{4,8},{8,12},{12,16},{16,20},{20,24},{24,28},{28,32},{32,36}... | collective-permute-start | bytes 14 | tf_op jit(solution)/shard_map/ppermute | solution.py:14
  29.5 0.0 copy-start.2
  29.5 7.6 %collective-permute-done.1 = bf16[1,128,1792]{2,1,0:T(8,128)(2,1)S(1)} collective-permute-done((bf16[1,128,1792]{2,1,0:T(8,128)(2,1)}, bf16[1,128,1792]{2,1,0:T(8,128)(2,1)S(1)}, u32[]{:S(2)}, u32[]{:S(2)}) %collective-permute-start.1) | collective-permute-done | bytes 458784 | tf_op jit(solution)/shard_map/ppermute | solution.py:14
  37.0 4.1 collective-permute-done
  41.1 1.2 pad_maximum_fusion
  42.3 0.0 copy-done.2
  42.3 0.3 fusion
  42.6 0.0 copy-done
  42.6 0.0 copy-start.1
  42.6 0.0 copy-start.3
  42.6 1.3 fusion.13
  43.9 0.0 all-reduce.4.cloned.1.call-update
  44.0 0.0 all-reduce.6.cloned.1.call-start
  44.0 0.0 collective-permute-done.3
  44.0 0.0 collective-permute-done.2
  44.0 1.4 maximum_convert_fusion
  45.5 0.1 convert_bitcast_fusion
  45.5 56.2 %all-reduce.4.cloned.1.call-done = f32[384,256]{1,0:T(8,128)} async-done(((f32[384,256]{1,0:T(8,128)}), f32[384,256]{1,0:T(8,128)}) %all-reduce.4.cloned.1.call-update) | async-done | bytes 393232 | tf_op jit(solution)/shard_map/psum | solution.py:40
  101.8 1.1 multiply_reduce_fusion
  102.9 0.0 copy-done.1
  102.9 0.0 copy-done.3
  102.9 1.9 fusion.4
  104.8 3.1 fusion.7
  107.9 0.0 all-reduce.6.cloned.1.call-update
  107.9 1.3 dynamic-slice
  109.3 359.0 %all-reduce.6.cloned.1.call-done = f32[256,1792]{1,0:T(8,128)} async-done(((f32[256,1792]{1,0:T(8,128)}), f32[256,1792]{1,0:T(8,128)}) %all-reduce.6.cloned.1.call-update) | async-done | bytes 1835024
  468.3 2.0 constant_dynamic-slice_fusion
  (3 shorter events, 0.0 us)
Async XLA Ops:
  7.2 35.5 %copy-start = (bf16[1792,256]{1,0:T(8,128)(2,1)S(1)}, bf16[1792,256]{1,0:T(8,128)(2,1)}, u32[]{:S(2)}) copy-start(bf16[1792,256]{1,0:T(8,128)(2,1)} %param.11) | copy-start | bytes 2752516
  7.2 94.6 %all-reduce.4.cloned.1.call-start = ((), (), s32[]{:S(2)}) async-start(), calls=%async_computation | async-start | bytes 786432 | tf_op jit(solution)/shard_map/psum | solution.py:40
  7.2 29.8 %collective-permute-start.1 = (bf16[1,128,1792]{2,1,0:T(8,128)(2,1)}, bf16[1,128,1792]{2,1,0:T(8,128)(2,1)S(1)}, u32[]{:S(2)}, u32[]{:S(2)}) collective-permute-start(bf16[1,128,1792]{2,1,0:T(8,128)(2,1)} %param.7), channel_id=1, source_target_pairs={{0,8},{4,12},{8,16},{12,20},{16,24},{20,28},{24,32},{28,36},{32,40... | collective-permute-start | bytes 1376264 | tf_op jit(solution)/shard_map/ppermute | solution.py:14
  11.6 29.5 %collective-permute-start = (bf16[1,128,1792]{2,1,0:T(8,128)(2,1)}, bf16[1,128,1792]{2,1,0:T(8,128)(2,1)S(1)}, u32[]{:S(2)}, u32[]{:S(2)}) collective-permute-start(bf16[1,128,1792]{2,1,0:T(8,128)(2,1)} %param.7), channel_id=1, source_target_pairs={{0,4},{4,8},{8,12},{12,16},{16,20},{20,24},{24,28},{28,32},{32,36}... | collective-permute-start | bytes 1376264 | tf_op jit(solution)/shard_map/ppermute | solution.py:14
  14.9 29.1 %collective-permute-start.3 = (bf16[1]{0:T(256)(128)(2,1)}, bf16[1]{0:T(256)(128)(2,1)}, u32[]{:S(2)}, u32[]{:S(2)}) collective-permute-start(bf16[1]{0:T(256)(128)(2,1)} %bitcast.3), channel_id=1, source_target_pairs={{0,8},{4,12},{8,16},{12,20},{16,24},{20,28},{24,32},{28,36},{32,40... | collective-permute-start | bytes 14 | tf_op jit(solution)/shard_map/ppermute | solution.py:14
  22.9 21.2 %collective-permute-start.2 = (bf16[1]{0:T(256)(128)(2,1)}, bf16[1]{0:T(256)(128)(2,1)}, u32[]{:S(2)}, u32[]{:S(2)}) collective-permute-start(bf16[1]{0:T(256)(128)(2,1)} %bitcast.2), channel_id=1, source_target_pairs={{0,4},{4,8},{8,12},{12,16},{16,20},{20,24},{24,28},{28,32},{32,36}... | collective-permute-start | bytes 14 | tf_op jit(solution)/shard_map/ppermute | solution.py:14
  29.5 12.8 %copy-start.2 = (f32[1792]{0:T(1024)S(1)}, f32[1792]{0:T(1024)}, u32[]{:S(2)}) copy-start(f32[1792]{0:T(1024)} %param.10) | copy-start | bytes 21508
  42.6 60.3 %copy-start.1 = (bf16[1,3,1,128,256]{4,3,2,1,0:T(8,128)(2,1)S(1)}, bf16[1,3,1,128,256]{4,3,2,1,0:T(8,128)(2,1)}, u32[]{:S(2)}) copy-start(bf16[1,3,1,128,256]{4,3,2,1,0:T(8,128)(2,1)} %param.13) | copy-start | bytes 589828
  42.6 60.3 %copy-start.3 = (f32[256]{0:T(256)S(1)}, f32[256]{0:T(256)}, u32[]{:S(2)}) copy-start(f32[256]{0:T(256)} %param.12) | copy-start | bytes 3076
  44.0 424.3 %all-reduce.6.cloned.1.call-start = ((), (), s32[]{:S(2)}) async-start(), calls=%async_computation.1 | async-start | bytes 3670016
Sparse Core Ops, SparseCore 0:
  44.1 57.6 all-reduce.3
  108.1 360.1 all-reduce.5
where the time goes:
time: 478 us; the launch traced here: 477 us
  waiting for transfers between devices  427 us (89%)
  starting transfers between devices  21 us (4%)
  between operations  15.4 us (3%)
  other arithmetic  6.02 us (1%)
    unnamed x3, waiting for transfers between devices  359 us
    psum x1, waiting for transfers between devices, panel_work(): summed = lax.psum(partial_value, 'tp')  56.2 us
    ppermute x4, starting transfers between devices, from_behind(): lax.ppermute(shard, axis, [(i, (i + by) % devices) for i in range(devices)])  20.9 us
    ppermute x4, waiting for transfers between devices, from_behind(): lax.ppermute(shard, axis, [(i, (i + by) % devices) for i in range(devices)])  11.7 us
  transfers between devices with their start and end apart: 6, of which 4 were waited for; matrix products, arithmetic and copies ran while one was open for 1% of the time, Pallas kernels for 0%

commit v1 on v0

v1 whole, which is shorter than its diff:
```python
import jax
import jax.numpy as jnp
from jax import lax
from jax.sharding import PartitionSpec as P

epsilon = 1e-06
Y, Z, C, X = "y", "z", "c", "x"
f32, bf16 = jnp.float32, jnp.bfloat16


def chip_shift(shard, by):
    devices = lax.axis_size((Y, Z, C))
    pairs = [(i, (i + 2 * by) % devices) for i in range(devices)]
    return lax.ppermute(shard, (Y, Z, C), pairs)


def finish(raw, gain_latent, cotangent_rows, valid_mask):
    rms_lat = jnp.sqrt(jnp.mean(raw * raw, axis=-1) + epsilon)
    unit_rows = raw / rms_lat[:, None]
    normed = (unit_rows * gain_latent * valid_mask[:, None]).astype(bf16)
    weighted = gain_latent * (cotangent_rows.astype(f32) * valid_mask[:, None])
    latent_grad = (
        weighted - unit_rows * jnp.mean(unit_rows * weighted, axis=-1, keepdims=True)
    ) / rms_lat[:, None]
    return normed, latent_grad.astype(bf16)


def body(hidden, routes, counts, gain_in, kv_down, gain_latent, cotangent):
    panel_len, width = hidden.shape[1], hidden.shape[2]
    latent_width = kv_down.shape[1]
    ny, nz, nc, nx = (lax.axis_size(a) for a in (Y, Z, C, X))
    core = lax.axis_index(C)
    route = routes[0, 0]
    count = counts[0, 0]
    cot = cotangent.reshape(3, panel_len, latent_width)

    with jax.named_scope("share_core"):
        pair_hidden = lax.all_gather(hidden[0], C, axis=0, tiled=True)
        pair_cot1 = lax.all_gather(cot[1], C, axis=0, tiled=False)
    with jax.named_scope("cotangent_back"):
        came = chip_shift(jnp.stack([pair_cot1[0], cot[2]]), -1)

    with jax.named_scope("project"):
        scaled = (pair_hidden.astype(f32) * gain_in).astype(bf16)
        own = (hidden[0].astype(f32) * gain_in).astype(bf16)
        partial_raw = jnp.dot(own, kv_down, preferred_element_type=f32)
        spread = jnp.broadcast_to(partial_raw, (nx,) + partial_raw.shape)
    with jax.named_scope("sum_x"):
        raw = jnp.sum(lax.all_to_all(spread, X, 0, 0), axis=0)

    with jax.named_scope("finish"):
        position = lax.broadcasted_iota(jnp.int32, (panel_len,), 0)
        valid_mask = (position < count).astype(f32)
        cot1 = jnp.where(core == 0, pair_cot1[1], came[0])
        picked = jnp.where(route == 0, cot[0], jnp.where(route == 1, cot1, came[1]))
        normed, backward = finish(raw, gain_latent, picked, valid_mask)
        none = jnp.zeros_like(normed)
        slot0, sent1, sent2 = (jnp.where(route == o, normed, none) for o in range(3))

    with jax.named_scope("share_backward"):
        pair = lax.all_gather(jnp.stack([backward, sent1]), C, axis=0, tiled=False)
    with jax.named_scope("latent_out"):
        arrived = chip_shift(jnp.stack([pair[1, 1], sent2]), 1)

    with jax.named_scope("gradient"):
        rows = latent_width // nc
        shape = (latent_width, rows)
        pick = (
            lax.broadcasted_iota(jnp.int32, shape, 0)
            == nc * lax.broadcasted_iota(jnp.int32, shape, 1) + core
        ).astype(bf16)
        pair_backward = pair[:, 0].reshape(nc * panel_len, latent_width)
        mine = jnp.dot(pair_backward, pick, preferred_element_type=f32).astype(bf16)
        total = lax.dot_general(
            mine, scaled, (((0,), (0,)), ((), ())), preferred_element_type=f32
        )
    with jax.named_scope("sum_y"):
        sent = total.astype(bf16).reshape(ny, nz, width)
        over_y = jnp.sum(lax.all_to_all(sent, Y, 0, 0).astype(f32), axis=0)
    with jax.named_scope("sum_z"):
        lanes = over_y.reshape(nz, width // 128, 128)
        over_z = jnp.sum(lax.all_to_all(lanes, Z, 0, 0), axis=0)
        gradient = over_z.reshape(1, width)

    slot1 = jnp.where(core == 0, arrived[0], pair[0, 1])
    latent = jnp.stack([slot0, slot1, arrived[1]]).reshape(cotangent.shape)
    return latent, gradient


def solution(mesh):
    shape = dict(mesh.shape)
    tp = shape["tp"]
    ny, nz = 8, 16
    nc = shape["dp"] // (ny * nz)
    split = jax.sharding.Mesh(mesh.devices.reshape(ny, nz, nc, tp), (Y, Z, C, X))
    dp = (Y, Z, C)
    in_specs = (
        P(dp, None, X),
        P(dp, None),
        P(dp, None),
        P(X),
        P(X, None),
        P(),
        P(dp, None, None, None, None),
    )
    out_specs = (P(dp, None, None, None, None), P(dp, X))
    return jax.shard_map(body, mesh=split, in_specs=in_specs, out_specs=out_specs, check_vma=False)
```

time: 478 us -> 86.9 us (0.18)
  the two profiles are of different devices: /device:TPU:30 before, /device:TPU:64 now
where the time goes in v1:
time: 86.9 us; the launch traced here: 86.4 us
  starting transfers between devices  36.9 us (42%)
  waiting for transfers between devices  34 us (39%)
  blocking collectives  6.49 us (7%)
  local copies, waits for them, and re-layouts  3.14 us (4%)
  matrix products  2.3 us (3%)
  between operations  2.17 us (2%)
  other arithmetic  1.44 us (2%)
    ppermute x2, starting transfers between devices, chip_shift(): return lax.ppermute(shard, (Y, Z, C), pairs)  16.1 us
    all_to_all x1, waiting for transfers between devices, body(): over_y = jnp.sum(lax.all_to_all(sent, Y, 0, 0).astype(f32), axis=0)  14.6 us
    all_to_all x1, starting transfers between devices, body(): over_z = jnp.sum(lax.all_to_all(lanes, Z, 0, 0), axis=0)  13.8 us
    all_to_all x1, waiting for transfers between devices, body(): over_z = jnp.sum(lax.all_to_all(lanes, Z, 0, 0), axis=0)  13.6 us
    all_to_all x1, waiting for transfers between devices, body(): raw = jnp.sum(lax.all_to_all(spread, X, 0, 0), axis=0)  5.81 us
    all_to_all x1, starting transfers between devices, body(): over_y = jnp.sum(lax.all_to_all(sent, Y, 0, 0).astype(f32), axis=0)  3.47 us
    all_to_all x1, starting transfers between devices, body(): raw = jnp.sum(lax.all_to_all(spread, X, 0, 0), axis=0)  3.47 us
    all_gather x1, blocking collectives, body(): pair_hidden = lax.all_gather(hidden[0], C, axis=0, tiled=True)  2.59 us
  transfers between devices with their start and end apart: 5, of which 3 were waited for; matrix products, arithmetic and copies ran while one was open for 4% of the time, Pallas kernels for 0%

profile of v1, /device:TPU:64, one launch (start us, length us, event | category | flops | bytes accessed | tf_op | source)
XLA Modules:
  0.0 86.4 jit_solution(12412409462935408279)
XLA Ops:
  0.6 0.0 copy-start
  0.6 0.0 copy-start.1
  0.7 1.0 %fusion.12 = (bf16[1,1,1,128,256]{4,3,2,1,0:T(8,128)(2,1)S(1)}, bf16[1,128,256]{2,1,0:T(8,128)(2,1)S(1)}) fusion(bf16[1,3,1,128,256]{4,3,2,1,0:T(8,128)(2,1)} %param.13), kind=kLoop, calls=%fused_computation.41 | loop fusion | bytes 262144 | tf_op jit(solution)/shard_map/share_core/slice | solution.py:39
  1.6 1.9 %all-gather = bf16[2,1,1,128,256]{4,3,2,1,0:T(8,128)(2,1)S(1)} all-gather(bf16[1,1,1,128,256]{4,3,2,1,0:T(8,128)(2,1)S(1)} %get-tuple-element.10), channel_id=2, replica_groups=mesh['y'=8,'z'=16,'c'=2,'x'=4] {'c'}, dimensions={0}, use_global_device_ids=true | all-gather | bytes 196608 | tf_op jit(solution)/shard_map/share_core/all_gather | solution.py:39
  3.6 14.2 %collective-permute-start = (bf16[2,128,256]{2,1,0:T(8,128)(2,1)S(1)}, bf16[2,128,256]{2,1,0:T(8,128)(2,1)S(1)}, u32[]{:S(2)}, u32[]{:S(2)}) collective-permute-start(bf16[2,128,256]{2,1,0:T(8,128)(2,1)S(1)} %pad_maximum_fusion), channel_id=1, source_target_pairs={{0,1016},{4,1020},{8,0},{12,4},{16,8},{20,12},{24,16},{28,20},{32,... | collective-permute-start | bytes 393224 | tf_op jit(solution)/shard_map/cotangent_back/ppermute | solution.py:14
  17.8 0.0 copy-done
  17.8 0.0 copy-done.1
  17.8 1.0 %fusion.5 = f32[128,256]{1,0:T(8,128)S(1)} fusion(bf16[1792,256]{1,0:T(8,128)(2,1)S(1)} %copy-done, bf16[1,128,1792]{2,1,0:T(8,128)(2,1)S(1)} %copy-done.1, f32[1792]{0:T(1024)} %param.10), kind=kOutput, calls=%fused_computation.9 | convolution fusion | flops 118128640 | bytes 1514496 | tf_op jit(solution)/shard_map/project/dot_general | solution.py:46
  18.8 0.8 broadcast_in_dim.4
  19.6 3.5 %all-to-all-start = ((f32[4,128,256]{2,1,0:T(8,128)}), f32[4,128,256]{2,1,0:T(8,128)S(1)}, u32[]{:S(2)}, u32[]{:S(2)}) async-start(f32[4,128,256]{2,1,0:T(8,128)} %broadcast_in_dim.4), calls=%async_computation | async-start | bytes 1048576 | tf_op jit(solution)/shard_map/sum_x/all_to_all | solution.py:49
  24.4 0.0 copy-start.4
  24.5 0.0 copy-start.2
  24.5 2.6 %all-gather.2 = bf16[1,256,1792]{2,1,0:T(8,128)(2,1)S(1)} all-gather(bf16[1,128,1792]{2,1,0:T(8,128)(2,1)S(1)} %copy-done.1), channel_id=4, replica_groups=mesh['y'=8,'z'=16,'c'=2,'x'=4] {'c'}, dimensions={1}, use_global_device_ids=true | all-gather | bytes 1376256 | tf_op jit(solution)/shard_map/share_core/all_gather | solution.py:38
  27.1 5.8 %all-to-all-done = f32[4,128,256]{2,1,0:T(8,128)S(1)} async-done(((f32[4,128,256]{2,1,0:T(8,128)}), f32[4,128,256]{2,1,0:T(8,128)S(1)}, u32[]{:S(2)}, u32[]{:S(2)}) %all-to-all-start) | async-done | bytes 524320 | tf_op jit(solution)/shard_map/sum_x/all_to_all | solution.py:49
  32.9 0.1 multiply_reduce_fusion.1
  33.0 0.0 copy-done.4
  33.0 0.1 broadcast_select_fusion.2
  33.2 0.0 collective-permute-done
  33.2 0.0 copy-done.2
  33.2 0.0 copy-start.3
  33.2 0.2 multiply_reduce_fusion
  33.4 0.1 divide_convert_fusion
  33.6 2.0 %all-gather.1 = bf16[4,128,256]{2,1,0:T(8,128)(2,1)S(1)} all-gather(bf16[2,128,256]{2,1,0:T(8,128)(2,1)S(1)} %pad_maximum_fusion.1), channel_id=3, replica_groups=mesh['y'=8,'z'=16,'c'=2,'x'=4] {'c'}, dimensions={0}, use_global_device_ids=true | all-gather | bytes 393216 | tf_op jit(solution)/shard_map/share_backward/all_gather | solution.py:61
  35.6 0.0 copy-done.3
  35.6 1.3 %convolution_convert_fusion = bf16[128,1792]{1,0:T(8,128)(2,1)} fusion(bf16[256,256]{1,0:T(8,128)(2,1)S(1)} %bitcast.66, bf16[1,256,1792]{2,1,0:T(8,128)(2,1)S(1)} %all-gather.2, f32[1792]{0:T(1024)S(1)} %copy-done.3, s32[128]{0:T(128)S(1)} %multiply_add_fusion), kind=kOutput, calls=%fused_computation | convolution fusion | flops 135888896 | bytes 1515008 | tf_op jit(solution)/shard_map/gradient/dot_general | solution.py:74
  36.9 3.5 %all-to-all-start.1 = ((bf16[8,16,1792]{2,1,0:T(8,128)(2,1)}), bf16[8,16,1792]{2,1,0:T(8,128)(2,1)S(1)}, u32[]{:S(2)}, u32[]{:S(2)}) async-start(bf16[8,16,1792]{2,1,0:T(8,128)(2,1)} %bitcast.19), calls=%async_computation.1 | async-start | bytes 917504 | tf_op jit(solution)/shard_map/sum_y/all_to_all | solution.py:79
  40.4 1.9 %collective-permute-start.1 = (bf16[2,128,256]{2,1,0:T(8,128)(2,1)S(1)}, bf16[2,128,256]{2,1,0:T(8,128)(2,1)S(1)}, u32[]{:S(2)}, u32[]{:S(2)}) collective-permute-start(bf16[2,128,256]{2,1,0:T(8,128)(2,1)S(1)} %pad_maximum_fusion.2), channel_id=1, source_target_pairs={{0,8},{4,12},{8,16},{12,20},{16,24},{20,28},{24,32},{28,36},{32,40... | collective-permute-start | bytes 393224 | tf_op jit(solution)/shard_map/latent_out/ppermute | solution.py:14
  42.3 14.6 %all-to-all-done.1 = bf16[8,16,1792]{2,1,0:T(8,128)(2,1)S(1)} async-done(((bf16[8,16,1792]{2,1,0:T(8,128)(2,1)}), bf16[8,16,1792]{2,1,0:T(8,128)(2,1)S(1)}, u32[]{:S(2)}, u32[]{:S(2)}) %all-to-all-start.1) | async-done | bytes 458784 | tf_op jit(solution)/shard_map/sum_y/all_to_all | solution.py:79
  57.0 0.1 convert_reduce_fusion
  57.0 0.7 reshape.323
  57.7 13.8 %all-to-all-start.2 = ((f32[16,14,128]{2,1,0:T(8,128)}), f32[16,14,128]{2,1,0:T(8,128)S(1)}, u32[]{:S(2)}, u32[]{:S(2)}) async-start(f32[16,14,128]{2,1,0:T(8,128)} %reshape.323), calls=%async_computation.2 | async-start | bytes 262144 | tf_op jit(solution)/shard_map/sum_z/all_to_all | solution.py:82
  71.5 0.0 collective-permute-done.1
  71.5 0.7 maximum_bitcast_fusion
  72.2 13.6 %all-to-all-done.2 = f32[16,14,128]{2,1,0:T(8,128)S(1)} async-done(((f32[16,14,128]{2,1,0:T(8,128)}), f32[16,14,128]{2,1,0:T(8,128)S(1)}, u32[]{:S(2)}, u32[]{:S(2)}) %all-to-all-start.2) | async-done | bytes 114720 | tf_op jit(solution)/shard_map/sum_z/all_to_all | solution.py:82
  85.8 0.6 copy.13
  (14 shorter events, 0.2 us)
Async XLA Ops:
  0.6 17.2 %copy-start = (bf16[1792,256]{1,0:T(8,128)(2,1)S(1)}, bf16[1792,256]{1,0:T(8,128)(2,1)}, u32[]{:S(2)}) copy-start(bf16[1792,256]{1,0:T(8,128)(2,1)} %param.11) | copy-start | bytes 2752516
  0.6 17.2 %copy-start.1 = (bf16[1,128,1792]{2,1,0:T(8,128)(2,1)S(1)}, bf16[1,128,1792]{2,1,0:T(8,128)(2,1)}, u32[]{:S(2)}) copy-start(bf16[1,128,1792]{2,1,0:T(8,128)(2,1)} %param.7) | copy-start | bytes 1376260
  3.6 29.6 %collective-permute-start = (bf16[2,128,256]{2,1,0:T(8,128)(2,1)S(1)}, bf16[2,128,256]{2,1,0:T(8,128)(2,1)S(1)}, u32[]{:S(2)}, u32[]{:S(2)}) collective-permute-start(bf16[2,128,256]{2,1,0:T(8,128)(2,1)S(1)} %pad_maximum_fusion), channel_id=1, source_target_pairs={{0,1016},{4,1020},{8,0},{12,4},{16,8},{20,12},{24,16},{28,20},{32,... | collective-permute-start | bytes 393224 | tf_op jit(solution)/shard_map/cotangent_back/ppermute | solution.py:14
  19.6 13.2 %all-to-all-start = ((f32[4,128,256]{2,1,0:T(8,128)}), f32[4,128,256]{2,1,0:T(8,128)S(1)}, u32[]{:S(2)}, u32[]{:S(2)}) async-start(f32[4,128,256]{2,1,0:T(8,128)} %broadcast_in_dim.4), calls=%async_computation | async-start | bytes 1048576 | tf_op jit(solution)/shard_map/sum_x/all_to_all | solution.py:49
  24.4 8.6 %copy-start.4 = (f32[256]{0:T(256)S(1)}, f32[256]{0:T(256)}, u32[]{:S(2)}) copy-start(f32[256]{0:T(256)} %param.12) | copy-start | bytes 3076
  24.5 8.7 %copy-start.2 = (bf16[1,3,1,128,256]{4,3,2,1,0:T(8,128)(2,1)S(1)}, bf16[1,3,1,128,256]{4,3,2,1,0:T(8,128)(2,1)}, u32[]{:S(2)}) copy-start(bf16[1,3,1,128,256]{4,3,2,1,0:T(8,128)(2,1)} %param.13) | copy-start | bytes 589828
  33.2 2.4 %copy-start.3 = (f32[1792]{0:T(1024)S(1)}, f32[1792]{0:T(1024)}, u32[]{:S(2)}) copy-start(f32[1792]{0:T(1024)} %param.10) | copy-start | bytes 21508
  36.9 20.1 %all-to-all-start.1 = ((bf16[8,16,1792]{2,1,0:T(8,128)(2,1)}), bf16[8,16,1792]{2,1,0:T(8,128)(2,1)S(1)}, u32[]{:S(2)}, u32[]{:S(2)}) async-start(bf16[8,16,1792]{2,1,0:T(8,128)(2,1)} %bitcast.19), calls=%async_computation.1 | async-start | bytes 917504 | tf_op jit(solution)/shard_map/sum_y/all_to_all | solution.py:79
  40.4 31.1 %collective-permute-start.1 = (bf16[2,128,256]{2,1,0:T(8,128)(2,1)S(1)}, bf16[2,128,256]{2,1,0:T(8,128)(2,1)S(1)}, u32[]{:S(2)}, u32[]{:S(2)}) collective-permute-start(bf16[2,128,256]{2,1,0:T(8,128)(2,1)S(1)} %pad_maximum_fusion.2), channel_id=1, source_target_pairs={{0,8},{4,12},{8,16},{12,20},{16,24},{20,28},{24,32},{28,36},{32,40... | collective-permute-start | bytes 393224 | tf_op jit(solution)/shard_map/latent_out/ppermute | solution.py:14
  57.7 28.1 %all-to-all-start.2 = ((f32[16,14,128]{2,1,0:T(8,128)}), f32[16,14,128]{2,1,0:T(8,128)S(1)}, u32[]{:S(2)}, u32[]{:S(2)}) async-start(f32[16,14,128]{2,1,0:T(8,128)} %reshape.323), calls=%async_computation.2 | async-start | bytes 262144 | tf_op jit(solution)/shard_map/sum_z/all_to_all | solution.py:82

commit v2 on v1

v2 whole, which is shorter than its diff:
```python
import jax
import jax.numpy as jnp
from jax import lax
from jax.sharding import PartitionSpec as P

epsilon = 1e-06
Y, Z, C, X = "y", "z", "c", "x"
f32, bf16 = jnp.float32, jnp.bfloat16


def along_dp(shard, by):
    devices = lax.axis_size((Y, Z, C))
    pairs = [(i, (i + by) % devices) for i in range(devices)]
    return lax.ppermute(shard, (Y, Z, C), pairs)


def mixed(rank, size):
    up, down = size // 2 + rank // 2, size // 2 - 1 - rank // 2
    odd = rank % 2
    return up * (1 - odd) + down * odd


def other_core(shard):
    return lax.ppermute(shard, C, [(0, 1), (1, 0)])


def finish(raw, gain_latent, cotangent_rows, valid_mask):
    rms_lat = jnp.sqrt(jnp.mean(raw * raw, axis=-1) + epsilon)
    unit_rows = raw / rms_lat[:, None]
    normed = (unit_rows * gain_latent * valid_mask[:, None]).astype(bf16)
    weighted = gain_latent * (cotangent_rows.astype(f32) * valid_mask[:, None])
    latent_grad = (
        weighted - unit_rows * jnp.mean(unit_rows * weighted, axis=-1, keepdims=True)
    ) / rms_lat[:, None]
    return normed, latent_grad.astype(bf16)


def body(hidden, routes, counts, gain_in, kv_down, gain_latent, cotangent):
    panel_len, width = hidden.shape[1], hidden.shape[2]
    latent_width = kv_down.shape[1]
    ny, nz, nc, nx = (lax.axis_size(a) for a in (Y, Z, C, X))
    core = lax.axis_index(C)
    route = routes[0, 0]
    count = counts[0, 0]
    cot = cotangent.reshape(3, panel_len, latent_width)

    with jax.named_scope("project"):
        own_scaled = (hidden[0].astype(f32) * gain_in).astype(bf16)
        partial_raw = jnp.dot(own_scaled, kv_down, preferred_element_type=f32)
        spread = jnp.broadcast_to(partial_raw, (nx,) + partial_raw.shape)
    with jax.named_scope("after_project"):
        spread, cot_none, cot_one, cot_two, hidden_sent = lax.optimization_barrier(
            (spread, cot[0], cot[1], cot[2], hidden[0])
        )
    with jax.named_scope("sum_x"):
        raw = jnp.sum(lax.all_to_all(spread, X, 0, 0), axis=0)
    with jax.named_scope("cotangent_back"):
        came1 = along_dp(cot_one, -1)
        came2 = along_dp(cot_two, -2)
    with jax.named_scope("share_hidden"):
        pair_hidden = other_core(hidden_sent)

    with jax.named_scope("finish"):
        position = lax.broadcasted_iota(jnp.int32, (panel_len,), 0)
        valid_mask = (position < count).astype(f32)
        picked = jnp.where(route == 0, cot_none, jnp.where(route == 1, came1, came2))
        normed, backward = finish(raw, gain_latent, picked, valid_mask)
        none = jnp.zeros_like(normed)
        slot0, sent1, sent2 = (jnp.where(route == o, normed, none) for o in range(3))

    with jax.named_scope("share_backward"):
        pair_backward = other_core(backward)

    with jax.named_scope("gradient"):
        rows = latent_width // nc
        shape = (latent_width, rows)
        place = lax.broadcasted_iota(jnp.int32, shape, 1)
        turned_row = mixed(place // nz, ny) * nz + place % nz
        pick = (
            lax.broadcasted_iota(jnp.int32, shape, 0)
            == nc * turned_row + core
        ).astype(bf16)

        def part(back, scaled):
            mine = jnp.dot(back, pick, preferred_element_type=f32).astype(bf16)
            return lax.dot_general(
                mine, scaled, (((0,), (0,)), ((), ())), preferred_element_type=f32
            )

        pair_scaled = (pair_hidden.astype(f32) * gain_in).astype(bf16)
        total = part(backward, own_scaled) + part(pair_backward, pair_scaled)
        sent = total.astype(bf16).reshape(ny, nz, width)
    with jax.named_scope("after_gradient"):
        sent, sent1, sent2 = lax.optimization_barrier((sent, sent1, sent2))
    with jax.named_scope("sum_y"):
        turned = [[int(mixed(r, ny)) for r in range(ny)]]
        came_y = lax.all_to_all(sent, Y, 0, 0, axis_index_groups=turned)
        over_y = jnp.sum(came_y.astype(f32), axis=0)
    with jax.named_scope("latent_out"):
        slot1 = along_dp(sent1, 1)
        slot2 = along_dp(sent2, 2)
    latent = jnp.stack([slot0, slot1, slot2]).reshape(cotangent.shape)
    with jax.named_scope("sum_z"):
        lanes = over_y.reshape(nz, width // 256, 256).astype(bf16)
        lanes, latent = lax.optimization_barrier((lanes, latent))
        over_z = jnp.sum(lax.all_to_all(lanes, Z, 0, 0).astype(f32), axis=0)
        gradient = over_z.reshape(1, width)

    return latent, gradient


def solution(mesh):
    shape = dict(mesh.shape)
    tp = shape["tp"]
    ny, nz = 8, 16
    nc = shape["dp"] // (ny * nz)
    split = jax.sharding.Mesh(mesh.devices.reshape(ny, nz, nc, tp), (Y, Z, C, X))
    dp = (Y, Z, C)
    in_specs = (
        P(dp, None, X),
        P(dp, None),
        P(dp, None),
        P(X),
        P(X, None),
        P(),
        P(dp, None, None, None, None),
    )
    out_specs = (P(dp, None, None, None, None), P(dp, X))
    return jax.shard_map(body, mesh=split, in_specs=in_specs, out_specs=out_specs, check_vma=False)
```

time: 86.9 us -> 78.4 us (0.902)
  the two profiles are of different devices: /device:TPU:64 before, /device:TPU:10 now
where the time goes in v2:
time: 78.4 us; the launch traced here: 77.9 us
  starting transfers between devices  43.2 us (55%)
  blocking collectives  15.5 us (20%)
  waiting for transfers between devices  9.06 us (12%)
  local copies, waits for them, and re-layouts  3.46 us (4%)
  matrix products  3.06 us (4%)
  between operations  2.15 us (3%)
  other arithmetic  1.48 us (2%)
    ppermute x4, starting transfers between devices, along_dp(): return lax.ppermute(shard, (Y, Z, C), pairs)  24.7 us
    all_to_all x1, blocking collectives, body(): over_z = jnp.sum(lax.all_to_all(lanes, Z, 0, 0).astype(f32), axis=0)  15.5 us
    all_to_all x1, starting transfers between devices, body(): came_y = lax.all_to_all(sent, Y, 0, 0, axis_index_groups=turned)  9.21 us
    ppermute x4, waiting for transfers between devices, along_dp(): return lax.ppermute(shard, (Y, Z, C), pairs)  6.33 us
    all_to_all x1, starting transfers between devices, body(): raw = jnp.sum(lax.all_to_all(spread, X, 0, 0), axis=0)  4.95 us
    ppermute x2, starting transfers between devices, other_core(): return lax.ppermute(shard, C, [(0, 1), (1, 0)])  4.33 us
    all_to_all x1, waiting for transfers between devices, body(): came_y = lax.all_to_all(sent, Y, 0, 0, axis_index_groups=turned)  2.39 us
    dot_general x2, matrix products, part(): lax.dot_general(mine, scaled, (((0,), (0,)), ((), ())), preferred_element...  1.75 us
  transfers between devices with their start and end apart: 8, of which 4 were waited for; matrix products, arithmetic and copies ran while one was open for 2% of the time, Pallas kernels for 0%

profile of v2, /device:TPU:10, one launch (start us, length us, event | category | flops | bytes accessed | tf_op | source)
XLA Modules:
  0.0 77.9 jit_solution(7612866875418846091)
XLA Ops:
  0.6 0.0 copy-start
  0.6 0.0 copy-start.2
  0.7 1.0 %slice_bitcast_fusion = (bf16[128,256]{1,0:T(8,128)(2,1)S(1)}, bf16[128,256]{1,0:T(8,128)(2,1)S(1)}, bf16[128,256]{1,0:T(8,128)(2,1)S(1)}) fusion(bf16[1,3,1,128,256]{4,3,2,1,0:T(8,128)(2,1)} %param.13), kind=kLoop, calls=%fused_computation.36 | loop fusion | bytes 393216 | tf_op jit(solution)/shard_map/after_project/squeeze | solution.py:53
  1.7 0.3 copy-done
  1.9 0.0 copy-done.2
  1.9 1.3 %fusion.3 = f32[128,256]{1,0:T(8,128)S(1)} fusion(bf16[1792,256]{1,0:T(8,128)(2,1)S(1)} %copy-done, f32[1792]{0:T(1024)S(1)} %copy-done.2, bf16[1,128,1792]{2,1,0:T(8,128)(2,1)} %param.7), kind=kOutput, calls=%fused_computation.8 | convolution fusion | flops 118128640 | bytes 1514496 | tf_op jit(solution)/shard_map/project/dot_general | solution.py:49
  3.2 0.8 %broadcast_in_dim.6 = f32[4,128,256]{2,1,0:T(8,128)} broadcast(f32[128,256]{1,0:T(8,128)S(1)} %fusion.3), dimensions={1,2} | broadcast | bytes 655360 | tf_op jit(solution)/shard_map/project/broadcast_in_dim | solution.py:50
  4.1 0.0 copy-start.1
  4.1 5.0 %all-to-all-start = ((f32[4,128,256]{2,1,0:T(8,128)}), f32[4,128,256]{2,1,0:T(8,128)S(1)}, u32[]{:S(2)}, u32[]{:S(2)}) async-start(f32[4,128,256]{2,1,0:T(8,128)} %broadcast_in_dim.6), calls=%async_computation | async-start | bytes 1048576 | tf_op jit(solution)/shard_map/sum_x/all_to_all | solution.py:56
  9.0 17.0 %collective-permute-start = (bf16[128,256]{1,0:T(8,128)(2,1)S(1)}, bf16[128,256]{1,0:T(8,128)(2,1)S(1)}, u32[]{:S(2)}, u32[]{:S(2)}) collective-permute-start(bf16[128,256]{1,0:T(8,128)(2,1)S(1)} %get-tuple-element.13), channel_id=1, source_target_pairs={{0,1020},{4,0},{8,4},{12,8},{16,12},{20,16},{24,20},{28,24},{32,28... | collective-permute-start | bytes 196616 | tf_op jit(solution)/shard_map/cotangent_back/ppermute | solution.py:14
  26.0 3.0 %collective-permute-start.1 = (bf16[128,256]{1,0:T(8,128)(2,1)S(1)}, bf16[128,256]{1,0:T(8,128)(2,1)S(1)}, u32[]{:S(2)}, u32[]{:S(2)}) collective-permute-start(bf16[128,256]{1,0:T(8,128)(2,1)S(1)} %get-tuple-element.14), channel_id=1, source_target_pairs={{0,1016},{4,1020},{8,0},{12,4},{16,8},{20,12},{24,16},{28,20},{32,... | collective-permute-start | bytes 196616 | tf_op jit(solution)/shard_map/cotangent_back/ppermute | solution.py:14
  29.1 0.0 copy-done.1
  29.1 2.1 %collective-permute-start.3 = (bf16[128,1792]{1,0:T(8,128)(2,1)S(1)}, bf16[128,1792]{1,0:T(8,128)(2,1)S(1)}, u32[]{:S(2)}, u32[]{:S(2)}) collective-permute-start(bf16[128,1792]{1,0:T(8,128)(2,1)S(1)} %bitcast.42), channel_id=1, source_target_pairs={{0,4},{4,0},{1,5},{5,1},{2,6},{6,2},{3,7},{7,3},{8,12},{12,8},{9,1... | collective-permute-start | bytes 1376264 | tf_op jit(solution)/shard_map/share_hidden/ppermute | solution.py:24
  32.5 0.0 all-to-all-done
  32.6 0.1 multiply_reduce_fusion.1
  32.7 0.0 collective-permute-done
  32.7 0.0 collective-permute-done.1
  32.7 0.0 copy-start.3
  32.8 0.7 copy-done.3
  33.4 0.2 multiply_reduce_fusion
  33.6 0.1 divide_convert_fusion
  33.8 2.2 %collective-permute-start.2 = (bf16[128,256]{1,0:T(8,128)(2,1)S(1)}, bf16[128,256]{1,0:T(8,128)(2,1)S(1)}, u32[]{:S(2)}, u32[]{:S(2)}) collective-permute-start(bf16[128,256]{1,0:T(8,128)(2,1)S(1)} %divide_convert_fusion), channel_id=1, source_target_pairs={{0,4},{4,0},{1,5},{5,1},{2,6},{6,2},{3,7},{7,3},{8,12},{12,8},{9,1... | collective-permute-start | bytes 196616 | tf_op jit(solution)/shard_map/share_backward/ppermute | solution.py:24
  36.0 0.5 fusion.1
  36.5 0.1 broadcast_select_fusion
  36.6 0.3 collective-permute-done.2
  36.9 0.0 collective-permute-done.3
  36.9 1.3 %fusion = bf16[128,1792]{1,0:T(8,128)(2,1)} fusion(f32[128,1792]{1,0:T(8,128)S(1)} %fusion.1, bf16[128,256]{1,0:T(8,128)(2,1)S(1)} %collective-permute-done.2, bf16[128,1792]{1,0:T(8,128)(2,1)S(1)} %collective-permute-done.3, f32[1792]{0:T(1024)S(1)} %copy-done.2, s32[]{:T(128)S(6)} %axis_index.15, s32[128]{0:T(128)S(1)} %get-tuple-element.34, ...), kind=kOutput, calls=%fused_computation.1 | convolution fusion | flops 69320704 | bytes 1910020 | tf_op jit(solution)/shard_map/gradient/dot_general | solution.py:86
  38.2 9.2 %all-to-all-start.1 = ((bf16[8,16,1792]{2,1,0:T(8,128)(2,1)}), bf16[8,16,1792]{2,1,0:T(8,128)(2,1)S(1)}, u32[]{:S(2)}, u32[]{:S(2)}) async-start(bf16[8,16,1792]{2,1,0:T(8,128)(2,1)} %bitcast.7), calls=%async_computation.1 | async-start | bytes 917504 | tf_op jit(solution)/shard_map/sum_y/all_to_all | solution.py:97
  47.4 1.9 %collective-permute-start.4 = (bf16[128,256]{1,0:T(8,128)(2,1)S(1)}, bf16[128,256]{1,0:T(8,128)(2,1)S(1)}, u32[]{:S(2)}, u32[]{:S(2)}) collective-permute-start(bf16[128,256]{1,0:T(8,128)(2,1)S(1)} %get-tuple-element.18), channel_id=1, source_target_pairs={{0,4},{4,8},{8,12},{12,16},{16,20},{20,24},{24,28},{28,32},{32,36}... | collective-permute-start | bytes 196616 | tf_op jit(solution)/shard_map/latent_out/ppermute | solution.py:14
  49.3 2.7 %collective-permute-start.5 = (bf16[128,256]{1,0:T(8,128)(2,1)S(1)}, bf16[128,256]{1,0:T(8,128)(2,1)S(1)}, u32[]{:S(2)}, u32[]{:S(2)}) collective-permute-start(bf16[128,256]{1,0:T(8,128)(2,1)S(1)} %get-tuple-element.19), channel_id=1, source_target_pairs={{0,8},{4,12},{8,16},{12,20},{16,24},{20,28},{24,32},{28,36},{32,40... | collective-permute-start | bytes 196616 | tf_op jit(solution)/shard_map/latent_out/ppermute | solution.py:14
  52.0 0.1 fusion.11
  52.2 3.0 %collective-permute-done.4 = bf16[128,256]{1,0:T(8,128)(2,1)S(1)} collective-permute-done((bf16[128,256]{1,0:T(8,128)(2,1)S(1)}, bf16[128,256]{1,0:T(8,128)(2,1)S(1)}, u32[]{:S(2)}, u32[]{:S(2)}) %collective-permute-start.4) | collective-permute-done | bytes 65568 | tf_op jit(solution)/shard_map/latent_out/ppermute | solution.py:14
  55.2 3.3 %collective-permute-done.5 = bf16[128,256]{1,0:T(8,128)(2,1)S(1)} collective-permute-done((bf16[128,256]{1,0:T(8,128)(2,1)S(1)}, bf16[128,256]{1,0:T(8,128)(2,1)S(1)}, u32[]{:S(2)}, u32[]{:S(2)}) %collective-permute-start.5) | collective-permute-done | bytes 65568 | tf_op jit(solution)/shard_map/latent_out/ppermute | solution.py:14
  58.5 0.7 maximum_bitcast_fusion
  59.2 2.4 %all-to-all-done.1 = bf16[8,16,1792]{2,1,0:T(8,128)(2,1)S(1)} async-done(((bf16[8,16,1792]{2,1,0:T(8,128)(2,1)}), bf16[8,16,1792]{2,1,0:T(8,128)(2,1)S(1)}, u32[]{:S(2)}, u32[]{:S(2)}) %all-to-all-start.1) | async-done | bytes 458784 | tf_op jit(solution)/shard_map/sum_y/all_to_all | solution.py:97
  61.6 0.1 reduce_sum.53
  61.6 0.1 convert_element_type.66
  61.7 15.5 %all_to_all.15 = bf16[16,7,256]{2,1,0:T(8,128)(2,1)S(1)} all-to-all(bf16[16,7,256]{2,1,0:T(8,128)(2,1)S(1)} %convert_element_type.66), channel_id=1, replica_groups=mesh['y'=8,'z'=16,'c'=2,'x'=4] {'z'}, dimensions={0} | all-to-all | bytes 114688 | tf_op jit(solution)/shard_map/sum_z/all_to_all | solution.py:106
  77.3 0.6 copy.10
  (8 shorter events, 0.1 us)
Async XLA Ops:
  0.6 1.3 %copy-start = (bf16[1792,256]{1,0:T(8,128)(2,1)S(1)}, bf16[1792,256]{1,0:T(8,128)(2,1)}, u32[]{:S(2)}) copy-start(bf16[1792,256]{1,0:T(8,128)(2,1)} %param.11) | copy-start | bytes 2752516
  0.6 1.3 %copy-start.2 = (f32[1792]{0:T(1024)S(1)}, f32[1792]{0:T(1024)}, u32[]{:S(2)}) copy-start(f32[1792]{0:T(1024)} %param.10) | copy-start | bytes 21508
  4.1 25.0 %copy-start.1 = (bf16[1,128,1792]{2,1,0:T(8,128)(2,1)S(1)}, bf16[1,128,1792]{2,1,0:T(8,128)(2,1)}, u32[]{:S(2)}) copy-start(bf16[1,128,1792]{2,1,0:T(8,128)(2,1)} %param.7) | copy-start | bytes 1376260
  4.1 28.5 %all-to-all-start = ((f32[4,128,256]{2,1,0:T(8,128)}), f32[4,128,256]{2,1,0:T(8,128)S(1)}, u32[]{:S(2)}, u32[]{:S(2)}) async-start(f32[4,128,256]{2,1,0:T(8,128)} %broadcast_in_dim.6), calls=%async_computation | async-start | bytes 1048576 | tf_op jit(solution)/shard_map/sum_x/all_to_all | solution.py:56
  9.0 23.7 %collective-permute-start = (bf16[128,256]{1,0:T(8,128)(2,1)S(1)}, bf16[128,256]{1,0:T(8,128)(2,1)S(1)}, u32[]{:S(2)}, u32[]{:S(2)}) collective-permute-start(bf16[128,256]{1,0:T(8,128)(2,1)S(1)} %get-tuple-element.13), channel_id=1, source_target_pairs={{0,1020},{4,0},{8,4},{12,8},{16,12},{20,16},{24,20},{28,24},{32,28... | collective-permute-start | bytes 196616 | tf_op jit(solution)/shard_map/cotangent_back/ppermute | solution.py:14
  26.0 6.7 %collective-permute-start.1 = (bf16[128,256]{1,0:T(8,128)(2,1)S(1)}, bf16[128,256]{1,0:T(8,128)(2,1)S(1)}, u32[]{:S(2)}, u32[]{:S(2)}) collective-permute-start(bf16[128,256]{1,0:T(8,128)(2,1)S(1)} %get-tuple-element.14), channel_id=1, source_target_pairs={{0,1016},{4,1020},{8,0},{12,4},{16,8},{20,12},{24,16},{28,20},{32,... | collective-permute-start | bytes 196616 | tf_op jit(solution)/shard_map/cotangent_back/ppermute | solution.py:14
  29.1 7.8 %collective-permute-start.3 = (bf16[128,1792]{1,0:T(8,128)(2,1)S(1)}, bf16[128,1792]{1,0:T(8,128)(2,1)S(1)}, u32[]{:S(2)}, u32[]{:S(2)}) collective-permute-start(bf16[128,1792]{1,0:T(8,128)(2,1)S(1)} %bitcast.42), channel_id=1, source_target_pairs={{0,4},{4,0},{1,5},{5,1},{2,6},{6,2},{3,7},{7,3},{8,12},{12,8},{9,1... | collective-permute-start | bytes 1376264 | tf_op jit(solution)/shard_map/share_hidden/ppermute | solution.py:24
  32.7 0.7 copy-start.3
  33.8 3.1 %collective-permute-start.2 = (bf16[128,256]{1,0:T(8,128)(2,1)S(1)}, bf16[128,256]{1,0:T(8,128)(2,1)S(1)}, u32[]{:S(2)}, u32[]{:S(2)}) collective-permute-start(bf16[128,256]{1,0:T(8,128)(2,1)S(1)} %divide_convert_fusion), channel_id=1, source_target_pairs={{0,4},{4,0},{1,5},{5,1},{2,6},{6,2},{3,7},{7,3},{8,12},{12,8},{9,1... | collective-permute-start | bytes 196616 | tf_op jit(solution)/shard_map/share_backward/ppermute | solution.py:24
  38.2 23.4 %all-to-all-start.1 = ((bf16[8,16,1792]{2,1,0:T(8,128)(2,1)}), bf16[8,16,1792]{2,1,0:T(8,128)(2,1)S(1)}, u32[]{:S(2)}, u32[]{:S(2)}) async-start(bf16[8,16,1792]{2,1,0:T(8,128)(2,1)} %bitcast.7), calls=%async_computation.1 | async-start | bytes 917504 | tf_op jit(solution)/shard_map/sum_y/all_to_all | solution.py:97
  47.4 7.8 %collective-permute-start.4 = (bf16[128,256]{1,0:T(8,128)(2,1)S(1)}, bf16[128,256]{1,0:T(8,128)(2,1)S(1)}, u32[]{:S(2)}, u32[]{:S(2)}) collective-permute-start(bf16[128,256]{1,0:T(8,128)(2,1)S(1)} %get-tuple-element.18), channel_id=1, source_target_pairs={{0,4},{4,8},{8,12},{12,16},{16,20},{20,24},{24,28},{28,32},{32,36}... | collective-permute-start | bytes 196616 | tf_op jit(solution)/shard_map/latent_out/ppermute | solution.py:14
  49.3 9.2 %collective-permute-start.5 = (bf16[128,256]{1,0:T(8,128)(2,1)S(1)}, bf16[128,256]{1,0:T(8,128)(2,1)S(1)}, u32[]{:S(2)}, u32[]{:S(2)}) collective-permute-start(bf16[128,256]{1,0:T(8,128)(2,1)S(1)} %get-tuple-element.19), channel_id=1, source_target_pairs={{0,8},{4,12},{8,16},{12,20},{16,24},{20,28},{24,32},{28,36},{32,40... | collective-permute-start | bytes 196616 | tf_op jit(solution)/shard_map/latent_out/ppermute | solution.py:14

commit v3 on v2

--- a/solution.py
+++ b/solution.py
@@ -14,10 +14,10 @@
     return lax.ppermute(shard, (Y, Z, C), pairs)
 
 
-def mixed(rank, size):
-    up, down = size // 2 + rank // 2, size // 2 - 1 - rank // 2
-    odd = rank % 2
-    return up * (1 - odd) + down * odd
+def ordered(rank, size):
+    half = size // 2
+    late = rank // half
+    return (half + rank) * (1 - late) + (size - 1 - rank) * late
 
 
 def other_core(shard):
@@ -57,6 +57,8 @@
     with jax.named_scope("cotangent_back"):
         came1 = along_dp(cot_one, -1)
         came2 = along_dp(cot_two, -2)
+        gain_rows = jnp.broadcast_to(gain_latent, (8, latent_width))
+        came1, gain_rows = lax.optimization_barrier((came1, gain_rows))
     with jax.named_scope("share_hidden"):
         pair_hidden = other_core(hidden_sent)
 
@@ -64,7 +66,7 @@
         position = lax.broadcasted_iota(jnp.int32, (panel_len,), 0)
         valid_mask = (position < count).astype(f32)
         picked = jnp.where(route == 0, cot_none, jnp.where(route == 1, came1, came2))
-        normed, backward = finish(raw, gain_latent, picked, valid_mask)
+        normed, backward = finish(raw, gain_rows[0], picked, valid_mask)
         none = jnp.zeros_like(normed)
         slot0, sent1, sent2 = (jnp.where(route == o, normed, none) for o in range(3))
 
@@ -75,7 +77,7 @@
         rows = latent_width // nc
         shape = (latent_width, rows)
         place = lax.broadcasted_iota(jnp.int32, shape, 1)
-        turned_row = mixed(place // nz, ny) * nz + place % nz
+        turned_row = ordered(place // nz, ny) * nz + place % nz
         pick = (
             lax.broadcasted_iota(jnp.int32, shape, 0)
             == nc * turned_row + core
@@ -93,7 +95,7 @@
     with jax.named_scope("after_gradient"):
         sent, sent1, sent2 = lax.optimization_barrier((sent, sent1, sent2))
     with jax.named_scope("sum_y"):
-        turned = [[int(mixed(r, ny)) for r in range(ny)]]
+        turned = [[int(ordered(r, ny)) for r in range(ny)]]
         came_y = lax.all_to_all(sent, Y, 0, 0, axis_index_groups=turned)
         over_y = jnp.sum(came_y.astype(f32), axis=0)
     with jax.named_scope("latent_out"):

time: 78.4 us -> 78.4 us (level)
  no operation moved by 1% of the time
where the time goes in v3:
time: 78.4 us; the launch traced here: 77.8 us
  starting transfers between devices  43.2 us (55%)
  blocking collectives  15.5 us (20%)
  waiting for transfers between devices  9.05 us (12%)
  local copies, waits for them, and re-layouts  3.44 us (4%)
  matrix products  3.06 us (4%)
  between operations  2.14 us (3%)
  other arithmetic  1.48 us (2%)
    ppermute x4, starting transfers between devices, along_dp(): return lax.ppermute(shard, (Y, Z, C), pairs)  24.7 us
    all_to_all x1, blocking collectives, body(): over_z = jnp.sum(lax.all_to_all(lanes, Z, 0, 0).astype(f32), axis=0)  15.5 us
    all_to_all x1, starting transfers between devices, body(): came_y = lax.all_to_all(sent, Y, 0, 0, axis_index_groups=turned)  9.21 us
    ppermute x4, waiting for transfers between devices, along_dp(): return lax.ppermute(shard, (Y, Z, C), pairs)  6.31 us
    all_to_all x1, starting transfers between devices, body(): raw = jnp.sum(lax.all_to_all(spread, X, 0, 0), axis=0)  4.95 us
    ppermute x2, starting transfers between devices, other_core(): return lax.ppermute(shard, C, [(0, 1), (1, 0)])  4.33 us
    all_to_all x1, waiting for transfers between devices, body(): came_y = lax.all_to_all(sent, Y, 0, 0, axis_index_groups=turned)  2.41 us
    dot_general x2, matrix products, part(): lax.dot_general(mine, scaled, (((0,), (0,)), ((), ())), preferred_element...  1.75 us
  transfers between devices with their start and end apart: 8, of which 4 were waited for; matrix products, arithmetic and copies ran while one was open for 2% of the time, Pallas kernels for 0%

profile of v3, /device:TPU:10, one launch (start us, length us, event | category | flops | bytes accessed | tf_op | source)
XLA Modules:
  0.0 77.8 jit_solution(2018034632890881052)
XLA Ops:
  0.6 0.0 copy-start
  0.6 0.0 copy-start.2
  0.7 1.0 %slice_bitcast_fusion = (bf16[128,256]{1,0:T(8,128)(2,1)S(1)}, bf16[128,256]{1,0:T(8,128)(2,1)S(1)}, bf16[128,256]{1,0:T(8,128)(2,1)S(1)}) fusion(bf16[1,3,1,128,256]{4,3,2,1,0:T(8,128)(2,1)} %param.13), kind=kLoop, calls=%fused_computation.45 | loop fusion | bytes 393216 | tf_op jit(solution)/shard_map/after_project/squeeze | solution.py:53
  1.7 0.3 copy-done
  1.9 0.0 copy-done.2
  1.9 1.3 %fusion.3 = f32[128,256]{1,0:T(8,128)S(1)} fusion(bf16[1792,256]{1,0:T(8,128)(2,1)S(1)} %copy-done, f32[1792]{0:T(1024)S(1)} %copy-done.2, bf16[1,128,1792]{2,1,0:T(8,128)(2,1)} %param.7), kind=kOutput, calls=%fused_computation.14 | convolution fusion | flops 118128640 | bytes 1514496 | tf_op jit(solution)/shard_map/project/dot_general | solution.py:49
  3.2 0.8 %broadcast_in_dim.8 = f32[4,128,256]{2,1,0:T(8,128)} broadcast(f32[128,256]{1,0:T(8,128)S(1)} %fusion.3), dimensions={1,2} | broadcast | bytes 655360 | tf_op jit(solution)/shard_map/project/broadcast_in_dim | solution.py:50
  4.1 0.0 copy-start.1
  4.1 5.0 %all-to-all-start = ((f32[4,128,256]{2,1,0:T(8,128)}), f32[4,128,256]{2,1,0:T(8,128)S(1)}, u32[]{:S(2)}, u32[]{:S(2)}) async-start(f32[4,128,256]{2,1,0:T(8,128)} %broadcast_in_dim.8), calls=%async_computation | async-start | bytes 1048576 | tf_op jit(solution)/shard_map/sum_x/all_to_all | solution.py:56
  9.0 17.0 %collective-permute-start = (bf16[128,256]{1,0:T(8,128)(2,1)S(1)}, bf16[128,256]{1,0:T(8,128)(2,1)S(1)}, u32[]{:S(2)}, u32[]{:S(2)}) collective-permute-start(bf16[128,256]{1,0:T(8,128)(2,1)S(1)} %get-tuple-element.14), channel_id=1, source_target_pairs={{0,1020},{4,0},{8,4},{12,8},{16,12},{20,16},{24,20},{28,24},{32,28... | collective-permute-start | bytes 196616 | tf_op jit(solution)/shard_map/cotangent_back/ppermute | solution.py:14
  26.0 3.0 %collective-permute-start.1 = (bf16[128,256]{1,0:T(8,128)(2,1)S(1)}, bf16[128,256]{1,0:T(8,128)(2,1)S(1)}, u32[]{:S(2)}, u32[]{:S(2)}) collective-permute-start(bf16[128,256]{1,0:T(8,128)(2,1)S(1)} %get-tuple-element.18), channel_id=1, source_target_pairs={{0,1016},{4,1020},{8,0},{12,4},{16,8},{20,12},{24,16},{28,20},{32,... | collective-permute-start | bytes 196616 | tf_op jit(solution)/shard_map/cotangent_back/ppermute | solution.py:14
  29.1 0.0 copy-done.1
  29.1 2.1 %collective-permute-start.3 = (bf16[128,1792]{1,0:T(8,128)(2,1)S(1)}, bf16[128,1792]{1,0:T(8,128)(2,1)S(1)}, u32[]{:S(2)}, u32[]{:S(2)}) collective-permute-start(bf16[128,1792]{1,0:T(8,128)(2,1)S(1)} %bitcast.43), channel_id=1, source_target_pairs={{0,4},{4,0},{1,5},{5,1},{2,6},{6,2},{3,7},{7,3},{8,12},{12,8},{9,1... | collective-permute-start | bytes 1376264 | tf_op jit(solution)/shard_map/share_hidden/ppermute | solution.py:24
  32.5 0.0 copy-start.3
  32.6 0.0 collective-permute-done
  32.6 0.6 copy-done.3
  33.2 0.0 all-to-all-done
  33.3 0.1 multiply_reduce_fusion.1
  33.4 0.0 collective-permute-done.1
  33.4 0.2 multiply_reduce_fusion
  33.6 0.1 divide_convert_fusion
  33.7 2.2 %collective-permute-start.2 = (bf16[128,256]{1,0:T(8,128)(2,1)S(1)}, bf16[128,256]{1,0:T(8,128)(2,1)S(1)}, u32[]{:S(2)}, u32[]{:S(2)}) collective-permute-start(bf16[128,256]{1,0:T(8,128)(2,1)S(1)} %divide_convert_fusion), channel_id=1, source_target_pairs={{0,4},{4,0},{1,5},{5,1},{2,6},{6,2},{3,7},{7,3},{8,12},{12,8},{9,1... | collective-permute-start | bytes 196616 | tf_op jit(solution)/shard_map/share_backward/ppermute | solution.py:24
  35.9 0.5 fusion.1
  36.4 0.1 broadcast_select_fusion
  36.5 0.3 collective-permute-done.2
  36.9 0.0 collective-permute-done.3
  36.9 1.3 %fusion = bf16[128,1792]{1,0:T(8,128)(2,1)} fusion(f32[128,1792]{1,0:T(8,128)S(1)} %fusion.1, bf16[128,256]{1,0:T(8,128)(2,1)S(1)} %collective-permute-done.2, bf16[128,1792]{1,0:T(8,128)(2,1)S(1)} %collective-permute-done.3, f32[1792]{0:T(1024)S(1)} %copy-done.2, s32[]{:T(128)S(6)} %axis_index.15, s32[128]{0:T(128)S(1)} %get-tuple-element.38, ...), kind=kOutput, calls=%fused_computation.1 | convolution fusion | flops 69189632 | bytes 1910020 | tf_op jit(solution)/shard_map/gradient/dot_general | solution.py:88
  38.1 9.2 %all-to-all-start.1 = ((bf16[8,16,1792]{2,1,0:T(8,128)(2,1)}), bf16[8,16,1792]{2,1,0:T(8,128)(2,1)S(1)}, u32[]{:S(2)}, u32[]{:S(2)}) async-start(bf16[8,16,1792]{2,1,0:T(8,128)(2,1)} %bitcast.8), calls=%async_computation.1 | async-start | bytes 917504 | tf_op jit(solution)/shard_map/sum_y/all_to_all | solution.py:99
  47.4 1.9 %collective-permute-start.4 = (bf16[128,256]{1,0:T(8,128)(2,1)S(1)}, bf16[128,256]{1,0:T(8,128)(2,1)S(1)}, u32[]{:S(2)}, u32[]{:S(2)}) collective-permute-start(bf16[128,256]{1,0:T(8,128)(2,1)S(1)} %get-tuple-element.22), channel_id=1, source_target_pairs={{0,4},{4,8},{8,12},{12,16},{16,20},{20,24},{24,28},{28,32},{32,36}... | collective-permute-start | bytes 196616 | tf_op jit(solution)/shard_map/latent_out/ppermute | solution.py:14
  49.3 2.7 %collective-permute-start.5 = (bf16[128,256]{1,0:T(8,128)(2,1)S(1)}, bf16[128,256]{1,0:T(8,128)(2,1)S(1)}, u32[]{:S(2)}, u32[]{:S(2)}) collective-permute-start(bf16[128,256]{1,0:T(8,128)(2,1)S(1)} %get-tuple-element.23), channel_id=1, source_target_pairs={{0,8},{4,12},{8,16},{12,20},{16,24},{20,28},{24,32},{28,36},{32,40... | collective-permute-start | bytes 196616 | tf_op jit(solution)/shard_map/latent_out/ppermute | solution.py:14
  52.0 0.1 fusion.20
  52.1 2.9 %collective-permute-done.4 = bf16[128,256]{1,0:T(8,128)(2,1)S(1)} collective-permute-done((bf16[128,256]{1,0:T(8,128)(2,1)S(1)}, bf16[128,256]{1,0:T(8,128)(2,1)S(1)}, u32[]{:S(2)}, u32[]{:S(2)}) %collective-permute-start.4) | collective-permute-done | bytes 65568 | tf_op jit(solution)/shard_map/latent_out/ppermute | solution.py:14
  55.0 3.4 %collective-permute-done.5 = bf16[128,256]{1,0:T(8,128)(2,1)S(1)} collective-permute-done((bf16[128,256]{1,0:T(8,128)(2,1)S(1)}, bf16[128,256]{1,0:T(8,128)(2,1)S(1)}, u32[]{:S(2)}, u32[]{:S(2)}) %collective-permute-start.5) | collective-permute-done | bytes 65568 | tf_op jit(solution)/shard_map/latent_out/ppermute | solution.py:14
  58.4 0.7 maximum_bitcast_fusion
  59.1 2.4 %all-to-all-done.1 = bf16[8,16,1792]{2,1,0:T(8,128)(2,1)S(1)} async-done(((bf16[8,16,1792]{2,1,0:T(8,128)(2,1)}), bf16[8,16,1792]{2,1,0:T(8,128)(2,1)S(1)}, u32[]{:S(2)}, u32[]{:S(2)}) %all-to-all-start.1) | async-done | bytes 458784 | tf_op jit(solution)/shard_map/sum_y/all_to_all | solution.py:99
  61.5 0.1 reduce_sum.53
  61.6 0.1 convert_element_type.66
  61.7 15.5 %all_to_all.15 = bf16[16,7,256]{2,1,0:T(8,128)(2,1)S(1)} all-to-all(bf16[16,7,256]{2,1,0:T(8,128)(2,1)S(1)} %convert_element_type.66), channel_id=1, replica_groups=mesh['y'=8,'z'=16,'c'=2,'x'=4] {'z'}, dimensions={0} | all-to-all | bytes 114688 | tf_op jit(solution)/shard_map/sum_z/all_to_all | solution.py:108
  77.2 0.6 copy.10
  (10 shorter events, 0.1 us)
Async XLA Ops:
  0.6 1.3 %copy-start = (bf16[1792,256]{1,0:T(8,128)(2,1)S(1)}, bf16[1792,256]{1,0:T(8,128)(2,1)}, u32[]{:S(2)}) copy-start(bf16[1792,256]{1,0:T(8,128)(2,1)} %param.11) | copy-start | bytes 2752516
  0.6 1.3 %copy-start.2 = (f32[1792]{0:T(1024)S(1)}, f32[1792]{0:T(1024)}, u32[]{:S(2)}) copy-start(f32[1792]{0:T(1024)} %param.10) | copy-start | bytes 21508
  4.1 25.0 %copy-start.1 = (bf16[1,128,1792]{2,1,0:T(8,128)(2,1)S(1)}, bf16[1,128,1792]{2,1,0:T(8,128)(2,1)}, u32[]{:S(2)}) copy-start(bf16[1,128,1792]{2,1,0:T(8,128)(2,1)} %param.7) | copy-start | bytes 1376260
  4.1 29.2 %all-to-all-start = ((f32[4,128,256]{2,1,0:T(8,128)}), f32[4,128,256]{2,1,0:T(8,128)S(1)}, u32[]{:S(2)}, u32[]{:S(2)}) async-start(f32[4,128,256]{2,1,0:T(8,128)} %broadcast_in_dim.8), calls=%async_computation | async-start | bytes 1048576 | tf_op jit(solution)/shard_map/sum_x/all_to_all | solution.py:56
  9.0 23.5 %collective-permute-start = (bf16[128,256]{1,0:T(8,128)(2,1)S(1)}, bf16[128,256]{1,0:T(8,128)(2,1)S(1)}, u32[]{:S(2)}, u32[]{:S(2)}) collective-permute-start(bf16[128,256]{1,0:T(8,128)(2,1)S(1)} %get-tuple-element.14), channel_id=1, source_target_pairs={{0,1020},{4,0},{8,4},{12,8},{16,12},{20,16},{24,20},{28,24},{32,28... | collective-permute-start | bytes 196616 | tf_op jit(solution)/shard_map/cotangent_back/ppermute | solution.py:14
  26.0 7.4 %collective-permute-start.1 = (bf16[128,256]{1,0:T(8,128)(2,1)S(1)}, bf16[128,256]{1,0:T(8,128)(2,1)S(1)}, u32[]{:S(2)}, u32[]{:S(2)}) collective-permute-start(bf16[128,256]{1,0:T(8,128)(2,1)S(1)} %get-tuple-element.18), channel_id=1, source_target_pairs={{0,1016},{4,1020},{8,0},{12,4},{16,8},{20,12},{24,16},{28,20},{32,... | collective-permute-start | bytes 196616 | tf_op jit(solution)/shard_map/cotangent_back/ppermute | solution.py:14
  29.1 7.8 %collective-permute-start.3 = (bf16[128,1792]{1,0:T(8,128)(2,1)S(1)}, bf16[128,1792]{1,0:T(8,128)(2,1)S(1)}, u32[]{:S(2)}, u32[]{:S(2)}) collective-permute-start(bf16[128,1792]{1,0:T(8,128)(2,1)S(1)} %bitcast.43), channel_id=1, source_target_pairs={{0,4},{4,0},{1,5},{5,1},{2,6},{6,2},{3,7},{7,3},{8,12},{12,8},{9,1... | collective-permute-start | bytes 1376264 | tf_op jit(solution)/shard_map/share_hidden/ppermute | solution.py:24
  32.5 0.7 copy-start.3
  33.7 3.1 %collective-permute-start.2 = (bf16[128,256]{1,0:T(8,128)(2,1)S(1)}, bf16[128,256]{1,0:T(8,128)(2,1)S(1)}, u32[]{:S(2)}, u32[]{:S(2)}) collective-permute-start(bf16[128,256]{1,0:T(8,128)(2,1)S(1)} %divide_convert_fusion), channel_id=1, source_target_pairs={{0,4},{4,0},{1,5},{5,1},{2,6},{6,2},{3,7},{7,3},{8,12},{12,8},{9,1... | collective-permute-start | bytes 196616 | tf_op jit(solution)/shard_map/share_backward/ppermute | solution.py:24
  38.1 23.4 %all-to-all-start.1 = ((bf16[8,16,1792]{2,1,0:T(8,128)(2,1)}), bf16[8,16,1792]{2,1,0:T(8,128)(2,1)S(1)}, u32[]{:S(2)}, u32[]{:S(2)}) async-start(bf16[8,16,1792]{2,1,0:T(8,128)(2,1)} %bitcast.8), calls=%async_computation.1 | async-start | bytes 917504 | tf_op jit(solution)/shard_map/sum_y/all_to_all | solution.py:99
  47.4 7.7 %collective-permute-start.4 = (bf16[128,256]{1,0:T(8,128)(2,1)S(1)}, bf16[128,256]{1,0:T(8,128)(2,1)S(1)}, u32[]{:S(2)}, u32[]{:S(2)}) collective-permute-start(bf16[128,256]{1,0:T(8,128)(2,1)S(1)} %get-tuple-element.22), channel_id=1, source_target_pairs={{0,4},{4,8},{8,12},{12,16},{16,20},{20,24},{24,28},{28,32},{32,36}... | collective-permute-start | bytes 196616 | tf_op jit(solution)/shard_map/latent_out/ppermute | solution.py:14
  49.3 9.2 %collective-permute-start.5 = (bf16[128,256]{1,0:T(8,128)(2,1)S(1)}, bf16[128,256]{1,0:T(8,128)(2,1)S(1)}, u32[]{:S(2)}, u32[]{:S(2)}) collective-permute-start(bf16[128,256]{1,0:T(8,128)(2,1)S(1)} %get-tuple-element.23), channel_id=1, source_target_pairs={{0,8},{4,12},{8,16},{12,20},{16,24},{20,28},{24,32},{28,36},{32,40... | collective-permute-start | bytes 196616 | tf_op jit(solution)/shard_map/latent_out/ppermute | solution.py:14

commit v4 on v3

--- a/solution.py
+++ b/solution.py
@@ -60,7 +60,7 @@
         gain_rows = jnp.broadcast_to(gain_latent, (8, latent_width))
         came1, gain_rows = lax.optimization_barrier((came1, gain_rows))
     with jax.named_scope("share_hidden"):
-        pair_hidden = other_core(hidden_sent)
+        pair_hidden = lax.all_gather(hidden_sent, C, axis=0, tiled=True)
 
     with jax.named_scope("finish"):
         position = lax.broadcasted_iota(jnp.int32, (panel_len,), 0)
@@ -71,7 +71,7 @@
         slot0, sent1, sent2 = (jnp.where(route == o, normed, none) for o in range(3))
 
     with jax.named_scope("share_backward"):
-        pair_backward = other_core(backward)
+        pair_backward = lax.all_gather(backward, C, axis=0, tiled=True)
 
     with jax.named_scope("gradient"):
         rows = latent_width // nc
@@ -90,7 +90,7 @@
             )
 
         pair_scaled = (pair_hidden.astype(f32) * gain_in).astype(bf16)
-        total = part(backward, own_scaled) + part(pair_backward, pair_scaled)
+        total = part(pair_backward, pair_scaled)
         sent = total.astype(bf16).reshape(ny, nz, width)
     with jax.named_scope("after_gradient"):
         sent, sent1, sent2 = lax.optimization_barrier((sent, sent1, sent2))

time: 78.4 us -> 77 us (0.982)
  starting transfers between devices: 43.2 us -> 38.9 us
  blocking collectives: 15.5 us -> 19.8 us
    all_gather x0 -> x2, blocking collectives: none -> 4.36 us  [the longest x1 2.46 us: body(): pair_hidden = lax.all_gather(hidden_sent, C, axis=0, tiled=True)]
    ppermute x2 -> x0, starting transfers between devices: 4.33 us -> none  [other_core(): return lax.ppermute(shard, C, [(0, 1), (1, 0)])]
    dot_general x2 -> x1, matrix products: 1.75 us -> 1.33 us  [part(): lax.dot_general(mine, scaled, (((0,), (0,)), ((), ())), preferred_element...]
  transfers between devices with their start and end apart: 8 -> 6, of which waited for: 4 -> 3; matrix products, arithmetic and copies ran while one was open for 2% -> 1% of each run, Pallas kernels for 0% -> 0%
where the time goes in v4:
time: 77 us; the launch traced here: 76.5 us
  starting transfers between devices  38.9 us (51%)
  blocking collectives  19.8 us (26%)
  waiting for transfers between devices  8.7 us (11%)
  local copies, waits for them, and re-layouts  2.81 us (4%)
  matrix products  2.65 us (3%)
  between operations  2.14 us (3%)
  other arithmetic  1.48 us (2%)
    ppermute x4, starting transfers between devices, along_dp(): return lax.ppermute(shard, (Y, Z, C), pairs)  24.9 us
    all_to_all x1, blocking collectives, body(): over_z = jnp.sum(lax.all_to_all(lanes, Z, 0, 0).astype(f32), axis=0)  15.5 us
    all_to_all x1, starting transfers between devices, body(): came_y = lax.all_to_all(sent, Y, 0, 0, axis_index_groups=turned)  9.22 us
    ppermute x4, waiting for transfers between devices, along_dp(): return lax.ppermute(shard, (Y, Z, C), pairs)  6.27 us
    all_to_all x1, starting transfers between devices, body(): raw = jnp.sum(lax.all_to_all(spread, X, 0, 0), axis=0)  4.83 us
    all_gather x1, blocking collectives, body(): pair_hidden = lax.all_gather(hidden_sent, C, axis=0, tiled=True)  2.46 us
    all_to_all x1, waiting for transfers between devices, body(): came_y = lax.all_to_all(sent, Y, 0, 0, axis_index_groups=turned)  2.42 us
    all_gather x1, blocking collectives, body(): pair_backward = lax.all_gather(backward, C, axis=0, tiled=True)  1.9 us
  transfers between devices with their start and end apart: 6, of which 3 were waited for; matrix products, arithmetic and copies ran while one was open for 1% of the time, Pallas kernels for 0%

profile of v4, /device:TPU:10, one launch (start us, length us, event | category | flops | bytes accessed | tf_op | source)
XLA Modules:
  0.0 76.5 jit_solution(5347798929280737035)
XLA Ops:
  0.6 0.0 copy-start
  0.6 1.0 %slice_bitcast_fusion = (bf16[128,256]{1,0:T(8,128)(2,1)S(1)}, bf16[128,256]{1,0:T(8,128)(2,1)S(1)}, bf16[128,256]{1,0:T(8,128)(2,1)S(1)}) fusion(bf16[1,3,1,128,256]{4,3,2,1,0:T(8,128)(2,1)} %param.13), kind=kLoop, calls=%fused_computation.57 | loop fusion | bytes 393216 | tf_op jit(solution)/shard_map/after_project/squeeze | solution.py:53
  1.6 0.3 copy-done
  1.9 1.3 %fusion.1 = f32[128,256]{1,0:T(8,128)S(1)} fusion(bf16[1792,256]{1,0:T(8,128)(2,1)S(1)} %copy-done, f32[1792]{0:T(1024)} %param.10, bf16[1,128,1792]{2,1,0:T(8,128)(2,1)} %param.7), kind=kOutput, calls=%fused_computation.5 | convolution fusion | flops 118128640 | bytes 1514496 | tf_op jit(solution)/shard_map/project/dot_general | solution.py:49
  3.2 0.0 copy-start.1
  3.3 0.8 %broadcast_in_dim.8 = f32[4,128,256]{2,1,0:T(8,128)} broadcast(f32[128,256]{1,0:T(8,128)S(1)} %fusion.1), dimensions={1,2} | broadcast | bytes 655360 | tf_op jit(solution)/shard_map/project/broadcast_in_dim | solution.py:50
  4.1 4.8 %all-to-all-start = ((f32[4,128,256]{2,1,0:T(8,128)}), f32[4,128,256]{2,1,0:T(8,128)S(1)}, u32[]{:S(2)}, u32[]{:S(2)}) async-start(f32[4,128,256]{2,1,0:T(8,128)} %broadcast_in_dim.8), calls=%async_computation | async-start | bytes 1048576 | tf_op jit(solution)/shard_map/sum_x/all_to_all | solution.py:56
  8.9 0.0 copy-start.3
  8.9 17.1 %collective-permute-start = (bf16[128,256]{1,0:T(8,128)(2,1)S(1)}, bf16[128,256]{1,0:T(8,128)(2,1)S(1)}, u32[]{:S(2)}, u32[]{:S(2)}) collective-permute-start(bf16[128,256]{1,0:T(8,128)(2,1)S(1)} %get-tuple-element.14), channel_id=1, source_target_pairs={{0,1020},{4,0},{8,4},{12,8},{16,12},{20,16},{24,20},{28,24},{32,28... | collective-permute-start | bytes 196616 | tf_op jit(solution)/shard_map/cotangent_back/ppermute | solution.py:14
  26.0 3.0 %collective-permute-start.1 = (bf16[128,256]{1,0:T(8,128)(2,1)S(1)}, bf16[128,256]{1,0:T(8,128)(2,1)S(1)}, u32[]{:S(2)}, u32[]{:S(2)}) collective-permute-start(bf16[128,256]{1,0:T(8,128)(2,1)S(1)} %get-tuple-element.18), channel_id=1, source_target_pairs={{0,1016},{4,1020},{8,0},{12,4},{16,8},{20,12},{24,16},{28,20},{32,... | collective-permute-start | bytes 196616 | tf_op jit(solution)/shard_map/cotangent_back/ppermute | solution.py:14
  30.4 0.0 copy-done.1
  30.4 2.5 %all_gather.7 = bf16[256,1792]{1,0:T(8,128)(2,1)S(1)} all-gather(bf16[128,1792]{1,0:T(8,128)(2,1)S(1)} %bitcast.38), channel_id=1, replica_groups=mesh['y'=8,'z'=16,'c'=2,'x'=4] {'c'}, dimensions={0}, use_global_device_ids=true | all-gather | bytes 1376256 | tf_op jit(solution)/shard_map/share_hidden/all_gather | solution.py:63
  32.9 0.0 collective-permute-done
  32.9 0.0 copy-done.3
  32.9 0.0 copy-start.2
  32.9 0.0 all-to-all-done
  33.0 0.1 multiply_reduce_fusion.1
  33.1 0.0 collective-permute-done.1
  33.1 0.2 multiply_reduce_fusion
  33.3 0.1 divide_convert_fusion
  33.5 1.9 %all_gather.6 = bf16[256,256]{1,0:T(8,128)(2,1)S(1)} all-gather(bf16[128,256]{1,0:T(8,128)(2,1)S(1)} %divide_convert_fusion), channel_id=1, replica_groups=mesh['y'=8,'z'=16,'c'=2,'x'=4] {'c'}, dimensions={0}, use_global_device_ids=true | all-gather | bytes 196608 | tf_op jit(solution)/shard_map/share_backward/all_gather | solution.py:74
  35.4 0.1 broadcast_select_fusion
  35.5 0.0 copy-done.2
  35.5 1.3 %convolution_convert_fusion = bf16[128,1792]{1,0:T(8,128)(2,1)} fusion(bf16[256,256]{1,0:T(8,128)(2,1)S(1)} %all_gather.6, bf16[256,1792]{1,0:T(8,128)(2,1)S(1)} %all_gather.7, f32[1792]{0:T(1024)S(1)} %copy-done.2, s32[]{:T(128)S(6)} %axis_index.15, s32[128]{0:T(128)S(1)} %get-tuple-element.38, s32[128]{0:T(128)S(1)} %get-tuple-element.39, ...), kind=kOutput, calls=%fused_computation | convolution fusion | flops 136773632 | bytes 1516804 | tf_op jit(solution)/shard_map/gradient/dot_general | solution.py:88
  36.8 9.2 %all-to-all-start.1 = ((bf16[8,16,1792]{2,1,0:T(8,128)(2,1)}), bf16[8,16,1792]{2,1,0:T(8,128)(2,1)S(1)}, u32[]{:S(2)}, u32[]{:S(2)}) async-start(bf16[8,16,1792]{2,1,0:T(8,128)(2,1)} %bitcast.8), calls=%async_computation.1 | async-start | bytes 917504 | tf_op jit(solution)/shard_map/sum_y/all_to_all | solution.py:99
  46.0 1.9 %collective-permute-start.2 = (bf16[128,256]{1,0:T(8,128)(2,1)S(1)}, bf16[128,256]{1,0:T(8,128)(2,1)S(1)}, u32[]{:S(2)}, u32[]{:S(2)}) collective-permute-start(bf16[128,256]{1,0:T(8,128)(2,1)S(1)} %get-tuple-element.22), channel_id=1, source_target_pairs={{0,4},{4,8},{8,12},{12,16},{16,20},{20,24},{24,28},{28,32},{32,36}... | collective-permute-start | bytes 196616 | tf_op jit(solution)/shard_map/latent_out/ppermute | solution.py:14
  47.9 2.8 %collective-permute-start.3 = (bf16[128,256]{1,0:T(8,128)(2,1)S(1)}, bf16[128,256]{1,0:T(8,128)(2,1)S(1)}, u32[]{:S(2)}, u32[]{:S(2)}) collective-permute-start(bf16[128,256]{1,0:T(8,128)(2,1)S(1)} %get-tuple-element.23), channel_id=1, source_target_pairs={{0,8},{4,12},{8,16},{12,20},{16,24},{20,28},{24,32},{28,36},{32,40... | collective-permute-start | bytes 196616 | tf_op jit(solution)/shard_map/latent_out/ppermute | solution.py:14
  50.7 0.1 fusion.27
  50.9 2.8 %collective-permute-done.2 = bf16[128,256]{1,0:T(8,128)(2,1)S(1)} collective-permute-done((bf16[128,256]{1,0:T(8,128)(2,1)S(1)}, bf16[128,256]{1,0:T(8,128)(2,1)S(1)}, u32[]{:S(2)}, u32[]{:S(2)}) %collective-permute-start.2) | collective-permute-done | bytes 65568 | tf_op jit(solution)/shard_map/latent_out/ppermute | solution.py:14
  53.7 3.4 %collective-permute-done.3 = bf16[128,256]{1,0:T(8,128)(2,1)S(1)} collective-permute-done((bf16[128,256]{1,0:T(8,128)(2,1)S(1)}, bf16[128,256]{1,0:T(8,128)(2,1)S(1)}, u32[]{:S(2)}, u32[]{:S(2)}) %collective-permute-start.3) | collective-permute-done | bytes 65568 | tf_op jit(solution)/shard_map/latent_out/ppermute | solution.py:14
  57.1 0.7 maximum_bitcast_fusion
  57.8 2.4 %all-to-all-done.1 = bf16[8,16,1792]{2,1,0:T(8,128)(2,1)S(1)} async-done(((bf16[8,16,1792]{2,1,0:T(8,128)(2,1)}), bf16[8,16,1792]{2,1,0:T(8,128)(2,1)S(1)}, u32[]{:S(2)}, u32[]{:S(2)}) %all-to-all-start.1) | async-done | bytes 458784 | tf_op jit(solution)/shard_map/sum_y/all_to_all | solution.py:99
  60.2 0.1 reduce_sum.53
  60.3 0.1 convert_element_type.62
  60.4 15.5 %all_to_all.15 = bf16[16,7,256]{2,1,0:T(8,128)(2,1)S(1)} all-to-all(bf16[16,7,256]{2,1,0:T(8,128)(2,1)S(1)} %convert_element_type.62), channel_id=1, replica_groups=mesh['y'=8,'z'=16,'c'=2,'x'=4] {'z'}, dimensions={0} | all-to-all | bytes 114688 | tf_op jit(solution)/shard_map/sum_z/all_to_all | solution.py:108
  75.9 0.6 copy.10
  (10 shorter events, 0.1 us)
Async XLA Ops:
  0.6 1.3 %copy-start = (bf16[1792,256]{1,0:T(8,128)(2,1)S(1)}, bf16[1792,256]{1,0:T(8,128)(2,1)}, u32[]{:S(2)}) copy-start(bf16[1792,256]{1,0:T(8,128)(2,1)} %param.11) | copy-start | bytes 2752516
  3.2 27.2 %copy-start.1 = (bf16[1,128,1792]{2,1,0:T(8,128)(2,1)S(1)}, bf16[1,128,1792]{2,1,0:T(8,128)(2,1)}, u32[]{:S(2)}) copy-start(bf16[1,128,1792]{2,1,0:T(8,128)(2,1)} %param.7) | copy-start | bytes 1376260
  4.1 28.9 %all-to-all-start = ((f32[4,128,256]{2,1,0:T(8,128)}), f32[4,128,256]{2,1,0:T(8,128)S(1)}, u32[]{:S(2)}, u32[]{:S(2)}) async-start(f32[4,128,256]{2,1,0:T(8,128)} %broadcast_in_dim.8), calls=%async_computation | async-start | bytes 1048576 | tf_op jit(solution)/shard_map/sum_x/all_to_all | solution.py:56
  8.9 24.0 %copy-start.3 = (f32[256]{0:T(256)S(1)}, f32[256]{0:T(256)}, u32[]{:S(2)}) copy-start(f32[256]{0:T(256)} %param.12) | copy-start | bytes 3076
  8.9 24.0 %collective-permute-start = (bf16[128,256]{1,0:T(8,128)(2,1)S(1)}, bf16[128,256]{1,0:T(8,128)(2,1)S(1)}, u32[]{:S(2)}, u32[]{:S(2)}) collective-permute-start(bf16[128,256]{1,0:T(8,128)(2,1)S(1)} %get-tuple-element.14), channel_id=1, source_target_pairs={{0,1020},{4,0},{8,4},{12,8},{16,12},{20,16},{24,20},{28,24},{32,28... | collective-permute-start | bytes 196616 | tf_op jit(solution)/shard_map/cotangent_back/ppermute | solution.py:14
  26.0 7.1 %collective-permute-start.1 = (bf16[128,256]{1,0:T(8,128)(2,1)S(1)}, bf16[128,256]{1,0:T(8,128)(2,1)S(1)}, u32[]{:S(2)}, u32[]{:S(2)}) collective-permute-start(bf16[128,256]{1,0:T(8,128)(2,1)S(1)} %get-tuple-element.18), channel_id=1, source_target_pairs={{0,1016},{4,1020},{8,0},{12,4},{16,8},{20,12},{24,16},{28,20},{32,... | collective-permute-start | bytes 196616 | tf_op jit(solution)/shard_map/cotangent_back/ppermute | solution.py:14
  32.9 2.5 %copy-start.2 = (f32[1792]{0:T(1024)S(1)}, f32[1792]{0:T(1024)}, u32[]{:S(2)}) copy-start(f32[1792]{0:T(1024)} %param.10) | copy-start | bytes 21508
  36.8 23.4 %all-to-all-start.1 = ((bf16[8,16,1792]{2,1,0:T(8,128)(2,1)}), bf16[8,16,1792]{2,1,0:T(8,128)(2,1)S(1)}, u32[]{:S(2)}, u32[]{:S(2)}) async-start(bf16[8,16,1792]{2,1,0:T(8,128)(2,1)} %bitcast.8), calls=%async_computation.1 | async-start | bytes 917504 | tf_op jit(solution)/shard_map/sum_y/all_to_all | solution.py:99
  46.0 7.7 %collective-permute-start.2 = (bf16[128,256]{1,0:T(8,128)(2,1)S(1)}, bf16[128,256]{1,0:T(8,128)(2,1)S(1)}, u32[]{:S(2)}, u32[]{:S(2)}) collective-permute-start(bf16[128,256]{1,0:T(8,128)(2,1)S(1)} %get-tuple-element.22), channel_id=1, source_target_pairs={{0,4},{4,8},{8,12},{12,16},{16,20},{20,24},{24,28},{28,32},{32,36}... | collective-permute-start | bytes 196616 | tf_op jit(solution)/shard_map/latent_out/ppermute | solution.py:14
  47.9 9.2 %collective-permute-start.3 = (bf16[128,256]{1,0:T(8,128)(2,1)S(1)}, bf16[128,256]{1,0:T(8,128)(2,1)S(1)}, u32[]{:S(2)}, u32[]{:S(2)}) collective-permute-start(bf16[128,256]{1,0:T(8,128)(2,1)S(1)} %get-tuple-element.23), channel_id=1, source_target_pairs={{0,8},{4,12},{8,16},{12,20},{16,24},{20,28},{24,32},{28,36},{32,40... | collective-permute-start | bytes 196616 | tf_op jit(solution)/shard_map/latent_out/ppermute | solution.py:14
